TPU v7x, 128 devices: a whole 4x4x4 slice. The times are simulated.
128 devices in a mesh: group: 64 (over z, y, x), blk: 2 (over core).
Axes of the slice: x: 4, y: 4, z: 4, core: 2. Of those that a mesh axis runs over, the one named last changes fastest.
Arguments:
- embeddings: bfloat16 [262144, 1024], P(('group', 'blk')), may hold values from -6 to 6
- cluster_ids: int32 [262144, 1], P(('group', 'blk')), may hold values from 0 to 255; in each aligned block of 2048 rows (0 to 2047, 2048 to 4095, ...) at most 16 rows name the same one
Outputs:
- nearest: float32 [262144], P(('group', 'blk'))
Inputs may be any that keep to these rules, and one draw needn't show every extreme that they name: `cluster_ids`: among the rows of one device no cluster is named more than 16 times, a bound that some block reaches.
All inputs are finite; a program needn't handle non-finite values.
Results may differ from a plain program's by a relative error of at most 0.0014.
Values may be sent and summed in bfloat16 or wider, within the bound.
No kernel may reach another device: no remote copies, remote signals or barrier semaphores. Data moves between devices by JAX's collectives and lax.ppermute only.
A program may use at most 128 MiB of HBM per device.

v0:
```python
import jax
import jax.numpy as jnp
from jax import lax
from jax.sharding import PartitionSpec as P

CL_GROUP = 4


def per_device(embeddings, cluster_ids):
    rows_dev, width = embeddings.shape
    groups = lax.axis_size("group")
    clusters = CL_GROUP * groups
    most = max(2, 2 * rows_dev // clusters)
    wide = embeddings.astype(jnp.float32)
    unit = (wide * lax.rsqrt(jnp.sum(wide * wide, axis=1, keepdims=True) + 1e-06)).astype(
        jnp.bfloat16
    )
    labels = cluster_ids[:, 0]
    onehot = (labels[:, None] == jnp.arange(clusters, dtype=jnp.int32)[None, :]).astype(jnp.int32)
    rank = jnp.sum((jnp.cumsum(onehot, axis=0) - 1) * onehot, axis=1)
    target = labels * most + rank
    outgoing = jnp.zeros((clusters * most, width), jnp.bfloat16).at[target].set(unit)
    outgoing = outgoing.reshape(groups, CL_GROUP, most, width)
    members = lax.all_to_all(outgoing, "group", split_axis=0, concat_axis=2, tiled=True)[0]
    span = members.shape[1]
    filled = jnp.any(members != 0, axis=-1)
    mine = lax.axis_index("blk")
    start_best = jnp.full((CL_GROUP, span), -1.0, jnp.float32)
    piece = lax.all_gather(members, "blk", axis=1, tiled=True)
    similar = jnp.einsum("kpd,kqd->kpq", members, piece, preferred_element_type=jnp.float32)
    piece_filled = jnp.any(piece != 0, axis=-1)
    column = jnp.arange(piece.shape[1], dtype=jnp.int32)
    row_ids = mine * span + jnp.arange(span, dtype=jnp.int32)
    keep = (
        filled[:, :, None] & piece_filled[:, None, :] & (row_ids[:, None] != column[None, :])[None]
    )
    best = jnp.maximum(start_best, jnp.max(jnp.where(keep, similar, -1.0), axis=2))
    results = lax.all_to_all(best[None], "group", split_axis=2, concat_axis=0, tiled=True)
    return results.reshape(-1)[target]


def solution(mesh):
    placed = (P(("group", "blk"), None), P(("group", "blk"), None))
    return jax.shard_map(
        per_device, mesh=mesh, in_specs=placed, out_specs=P(("group", "blk")), check_vma=False
    )
```

profile of v0, /device:TPU:1, one launch (start us, length us, event | category | flops | bytes accessed | tf_op | source)
XLA Modules:
  0.0 262.6 jit_solution(6089532283520423202)
XLA Ops:
  6.5 0.0 copy-start
  6.5 0.0 all-gather.2.cloned.1.call-start
  6.5 3.1 %fusion = f32[2048]{0:T(1024)S(1)} fusion(bf16[2048,1024]{1,0:T(8,128)(2,1)} %param.2), kind=kLoop, calls=%fused_computation.7 | loop fusion | flops 6289408 | bytes 4202496 | tf_op jit(solution)/shard_map/reduce_sum | solution.py:15
  9.6 0.8 copy.14
  10.4 0.3 fusion.7
  10.8 0.3 add_add_fusion
  11.1 1.2 copy.15
  12.3 0.0 copy-done
  12.3 0.9 fusion.6
  13.3 15.8 %scatter_custom_fusion = bf16[4096,1024]{1,0:T(8,128)(2,1)} fusion(s32[2048]{0:T(1024)S(1)} %bitcast.36, bf16[2048,1024]{1,0:T(8,128)(2,1)} %param.2, f32[2048]{0:T(1024)S(1)} %add_rsqrt_fusion, bf16[]{:T(256)} %constant.12.clone.1), kind=kCustom, calls=%fused_computation.10 | custom fusion | flops 6291456 | bytes 12591106 | tf_op jit(solution)/shard_map/scatter | solution.py:22
  29.1 108.6 %all_to_all.30 = bf16[64,4,16,1024]{3,2,1,0:T(8,128)(2,1)} all-to-all(bf16[64,4,16,1024]{3,2,1,0:T(8,128)(2,1)} %bitcast.30), channel_id=1, replica_groups=mesh['group'=64,'blk'=2] {'group'}, dimensions={0} | all-to-all | bytes 16777216 | tf_op jit(solution)/shard_map/all_to_all | solution.py:24
  137.7 8.5 %copy.17 = bf16[1,4,64,16,1024]{4,3,2,1,0:T(8,128)(2,1)} copy(bf16[1,4,64,16,1024]{4,3,1,2,0:T(8,128)(2,1)} %bitcast.27) | data formatting | bytes 16777216 | tf_op jit(solution)/shard_map/all_to_all | solution.py:24
  146.2 0.0 all-gather.2.cloned.1.call-update
  146.3 1.7 iota_compare_fusion
  148.0 7.8 %compare_reduce_fusion.1 = pred[4,64,16]{2,0,1:T(4,128)(4,1)S(1)} fusion(bf16[64,4,16,1024]{3,2,1,0:T(8,128)(2,1)} %all_to_all.30), kind=kLoop, calls=%fused_computation.4 | loop fusion | flops 8384512 | bytes 8392704 | tf_op jit(solution)/shard_map/reduce_or | solution.py:26
  155.8 0.1 and.24
  156.0 23.0 %all-gather.2.cloned.1.call-done = bf16[4,2048,1024]{2,1,0:T(8,128)(2,1)} async-done(((bf16[4,1024,1024]{2,1,0:T(8,128)(2,1)}), bf16[4,2048,1024]{2,1,0:T(8,128)(2,1)}) %all-gather.2.cloned.1.call-update) | async-done | bytes 16777232 | tf_op jit(solution)/shard_map/all_gather | solution.py:29
  179.0 7.4 %compare_reduce_fusion = pred[4,2048]{1,0:T(4,128)(4,1)S(1)} fusion(bf16[4,2048,1024]{2,1,0:T(8,128)(2,1)} %all-gather.2.cloned.1.call-done), kind=kLoop, calls=%fused_computation.3 | loop fusion | flops 16769024 | bytes 16785408 | tf_op jit(solution)/shard_map/reduce_or | solution.py:31
  186.3 24.3 %select_reduce_fusion = f32[4,1024]{1,0:T(4,128)S(1)} fusion(bf16[4,1024,1024]{2,1,0:T(8,128)(2,1)} %bitcast.29, bf16[4,2048,1024]{2,1,0:T(8,128)(2,1)} %all-gather.2.cloned.1.call-done, pred[1024,2048]{1,0:T(8,128)(4,1)S(1)} %iota_compare_fusion, pred[4,2048]{1,0:T(4,128)(4,1)S(1)} %compare_reduce_fusion, pred[4,1024]{1,0:T(4,128)(4,1)S(1)} %and.24), kind=kOutput, calls=%fused_computation.2 | convolution fusion | flops 17213419520 | bytes 27291648 | tf_op jit(solution)/shard_map/kpd,kqd->kpq/dot_general | solution.py:30
  210.7 1.0 copy.18
  211.7 10.1 %all-to-all-start.1 = ((f32[1,4,1024]{1,0,2:T(1,128)}), f32[1,4,1024]{1,0,2:T(1,128)S(1)}, u32[]{:S(2)}, u32[]{:S(2)}) async-start(f32[1,4,1024]{1,0,2:T(1,128)} %copy.18), calls=%async_computation.1 | async-start | bytes 1048576 | tf_op jit(solution)/shard_map/all_to_all | solution.py:38
  221.8 12.6 %all-to-all-done.1 = f32[1,4,1024]{1,0,2:T(1,128)S(1)} async-done(((f32[1,4,1024]{1,0,2:T(1,128)}), f32[1,4,1024]{1,0,2:T(1,128)S(1)}, u32[]{:S(2)}, u32[]{:S(2)}) %all-to-all-start.1) | async-done | bytes 16416 | tf_op jit(solution)/shard_map/all_to_all | solution.py:38
  234.5 0.5 copy.21
  235.0 0.1 copy.20
  235.1 0.1 reshape.71
  235.2 20.5 %gather_fusion = f32[2048]{0:T(1024)} fusion(f32[4096]{0:T(1024)S(1)} %reshape.71, s32[2048]{0:T(1024)S(1)} %broadcast_clamp_fusion), kind=kCustom, calls=%fused_computation | custom fusion | bytes 24576 | tf_op jit(solution)/shard_map/gather | solution.py:39
  (9 shorter events, 0.1 us)
Async XLA Ops:
  6.5 5.8 %copy-start = (s32[2048,1]{0,1:T(1,128)S(1)}, s32[2048,1]{0,1:T(1,128)}, u32[]{:S(2)}) copy-start(s32[2048,1]{0,1:T(1,128)} %param.3) | copy-start | bytes 24580
  6.5 172.4 %all-gather.2.cloned.1.call-start = ((), (), s32[]{:S(2)}) async-start(), calls=%async_computation.2 | async-start | bytes 25165824 | tf_op jit(solution)/shard_map/all_gather | solution.py:29
  211.7 22.8 %all-to-all-start.1 = ((f32[1,4,1024]{1,0,2:T(1,128)}), f32[1,4,1024]{1,0,2:T(1,128)S(1)}, u32[]{:S(2)}, u32[]{:S(2)}) async-start(f32[1,4,1024]{1,0,2:T(1,128)} %copy.18), calls=%async_computation.1 | async-start | bytes 1048576 | tf_op jit(solution)/shard_map/all_to_all | solution.py:38
Sparse Core Ops, SparseCore 0:
  146.4 32.5 all-gather.1
where the time goes:
time: 263 us
  blocking collectives  109 us (41%)
  other arithmetic  37.4 us (14%)
  waiting for transfers between devices  35.6 us (14%)
  local copies, waits for them, and re-layouts  33 us (13%)
  matrix products  24.3 us (9%)
  between operations  13.5 us (5%)
  starting transfers between devices  10.1 us (4%)
    all_to_all x1, blocking collectives, per_device(): lax.all_to_all(outgoing, 'group', split_axis=0, concat_axis=2, tiled=True)  109 us
    dot_general x1, matrix products, per_device(): jnp.einsum('kpd,kqd->kpq', members, piece, preferred_element_type=jnp.flo...  24.3 us
    all_gather x1, waiting for transfers between devices, per_device(): piece = lax.all_gather(members, 'blk', axis=1, tiled=True)  23 us
    gather x1, local copies, waits for them, and re-layouts, per_device(): return results.reshape(-1)[target]  20.5 us
    scatter x1, other arithmetic, per_device(): jnp.zeros((clusters * most, width), jnp.bfloat16).at[target].set(unit)  15.8 us
    all_to_all x1, waiting for transfers between devices, per_device(): lax.all_to_all(best[None], 'group', split_axis=2, concat_axis=0, tiled=True)  12.6 us
    all_to_all x1, starting transfers between devices, per_device(): lax.all_to_all(best[None], 'group', split_axis=2, concat_axis=0, tiled=True)  10.1 us
    all_to_all x1, local copies, waits for them, and re-layouts, per_device(): lax.all_to_all(outgoing, 'group', split_axis=0, concat_axis=2, tiled=True)  8.51 us
  transfers between devices with their start and end apart: 2, of which 2 were waited for; matrix products, arithmetic and copies ran while one was open for 4% of the time, Pallas kernels for 0%

commit v1 on v0

v1 whole, which is shorter than its diff:
```python
import jax
import jax.numpy as jnp
from jax import lax
from jax.experimental import pallas as pl
from jax.experimental.pallas import tpu as pltpu
from jax.sharding import PartitionSpec as P

CLUSTERS = 256
MOST = 16
PAD = 2.0
LANES = 128


def prep_kernel(x_hbm, label_ref, out_hbm, target_ref, xbuf, at_ref, rows, slots, obuf, where, in_sem, out_sem, where_sem):
    n, width = x_hbm.shape
    chunks = width // LANES
    total = out_hbm.shape[0]
    clusters = total // MOST
    parts = in_sem.shape[0]
    step = n // parts
    loads = [
        pltpu.make_async_copy(x_hbm.at[pl.ds(p * step, step)], xbuf.at[pl.ds(p * step, step)], in_sem.at[p])
        for p in range(parts)
    ]
    for load in loads:
        load.start()

    span = 256
    before = (
        lax.broadcasted_iota(jnp.int32, (span, span), 0) < lax.broadcasted_iota(jnp.int32, (span, span), 1)
    ).astype(jnp.bfloat16)
    carry = jnp.zeros((clusters, 1), jnp.float32)
    cluster = lax.broadcasted_iota(jnp.int32, (clusters, span), 0)
    for b in range(n // span):
        label = label_ref[:, b * span : (b + 1) * span]
        hit = cluster == label
        hot = jnp.where(hit, 1.0, 0.0)
        count = jnp.dot(hot.astype(jnp.bfloat16), before, preferred_element_type=jnp.float32) + carry
        rank = jnp.sum(jnp.where(hit, count, 0.0), axis=0, keepdims=True)
        carry = carry + jnp.sum(hot, axis=1, keepdims=True)
        target = label * MOST + rank.astype(jnp.int32)
        target_ref[:, b * span : (b + 1) * span] = target
        at_ref[:, b * span : (b + 1) * span] = (target // 8) * (8 * chunks) + target % 8
    place = pltpu.make_async_copy(at_ref, where, where_sem)
    place.start()

    def fill(i, _):
        base = pl.multiple_of(i * 64 * chunks, 64 * chunks)
        slots[pl.ds(base, 64 * chunks), :] = jnp.full((64 * chunks, LANES), PAD, jnp.float32)
        return 0

    lax.fori_loop(0, total // 64, fill, 0)

    for p in range(parts):
        loads[p].wait()

        def unit(i, _):
            r = pl.multiple_of(p * step + i * 16, 16)
            wide = xbuf[pl.ds(r, 16), :].astype(jnp.float32)
            scaled = wide * lax.rsqrt(jnp.sum(wide * wide, axis=1, keepdims=True) + 1e-06)
            base = pl.multiple_of(r * chunks, 16 * chunks)
            for h in range(2):
                for c in range(chunks):
                    rows[pl.ds(base + (h * chunks + c) * 8, 8), :] = scaled[h * 8 : h * 8 + 8, c * LANES : (c + 1) * LANES]
            return 0

        lax.fori_loop(0, step // 16, unit, 0, unroll=8)
    place.wait()

    def move(i, _):
        got = [rows[pl.ds(i * 16 * chunks + (u // 8) * 8 * chunks + u % 8, chunks, stride=8), :] for u in range(16)]
        for u in range(16):
            slots[pl.ds(where[0, i * 16 + u], chunks, stride=8), :] = got[u]
        return 0

    lax.fori_loop(0, n // 16, move, 0, unroll=8)

    oparts = out_sem.shape[0]
    ostep = total // oparts
    stores = []
    for p in range(oparts):

        def pack(i, _):
            r = pl.multiple_of(p * ostep + i * 16, 16)
            base = pl.multiple_of(r * chunks, 16 * chunks)
            lo = [slots[pl.ds(base + c * 8, 8), :] for c in range(chunks)]
            hi = [slots[pl.ds(base + (chunks + c) * 8, 8), :] for c in range(chunks)]
            both = [jnp.concatenate([a, b], axis=0).astype(jnp.bfloat16) for a, b in zip(lo, hi)]
            for c in range(chunks):
                obuf[pl.ds(r, 16), c * LANES : (c + 1) * LANES] = both[c]
            return 0

        lax.fori_loop(0, ostep // 16, pack, 0, unroll=8)
        store = pltpu.make_async_copy(obuf.at[pl.ds(p * ostep, ostep)], out_hbm.at[pl.ds(p * ostep, ostep)], out_sem.at[p])
        store.start()
        stores.append(store)
    for store in stores:
        store.wait()


def prep(x, labels, clusters):
    n, width = x.shape
    total = clusters * MOST
    chunks = width // LANES
    return pl.pallas_call(
        prep_kernel,
        out_shape=(
            jax.ShapeDtypeStruct((total, width), jnp.bfloat16),
            jax.ShapeDtypeStruct((1, n), jnp.int32),
        ),
        in_specs=[pl.BlockSpec(memory_space=pl.ANY), pl.BlockSpec(memory_space=pltpu.VMEM)],
        out_specs=(pl.BlockSpec(memory_space=pl.ANY), pl.BlockSpec(memory_space=pltpu.VMEM)),
        scratch_shapes=[
            pltpu.VMEM((n, width), jnp.bfloat16),
            pltpu.VMEM((1, n), jnp.int32),
            pltpu.VMEM((n * chunks, LANES), jnp.float32),
            pltpu.VMEM((total * chunks, LANES), jnp.float32),
            pltpu.VMEM((total, width), jnp.bfloat16),
            pltpu.SMEM((1, n), jnp.int32),
            pltpu.SemaphoreType.DMA((8,)),
            pltpu.SemaphoreType.DMA((8,)),
            pltpu.SemaphoreType.DMA(()),
        ],
        compiler_params=pltpu.CompilerParams(vmem_limit_bytes=52 * 1024 * 1024),
        name="prep",
    )(x, labels)


def near_kernel(x_hbm, out_ref, rows, bias, row_best, col_best, packed, sem):
    sources, pair, width = x_hbm.shape
    per = pair // MOST
    n = sources * MOST
    tile = 256
    blocks = n // tile
    src_tile = tile // MOST
    loads = [
        [
            pltpu.make_async_copy(
                x_hbm.at[pl.ds(b * src_tile, src_tile), pl.ds(k * MOST, MOST), :],
                rows.at[k, pl.ds(b * src_tile, src_tile)],
                sem.at[k, b],
            )
            for b in range(blocks)
        ]
        for k in range(per)
    ]
    for k in range(per):
        for b in range(blocks):
            loads[k][b].start()
    first = (lax.broadcasted_iota(jnp.int32, (8, LANES), 1) == 0).astype(jnp.bfloat16)
    contract = (((1,), (1,)), ((), ()))
    diagonal = lax.broadcasted_iota(jnp.int32, (tile, tile), 0) == lax.broadcasted_iota(jnp.int32, (tile, tile), 1)
    for k in range(per):
        for b in range(blocks):
            loads[k][b].wait()
            mine = rows[k, b * src_tile : (b + 1) * src_tile].reshape(tile, width)
            mark = lax.dot_general(first, mine[:, :LANES], contract, preferred_element_type=jnp.float32)[0:1]
            col_bias = jnp.where(mark > 1.5, -1000.0, 0.0)
            row_mark = mine[:, 0:1].astype(jnp.float32)
            bias[b * tile : (b + 1) * tile, :] = jnp.broadcast_to(jnp.where(row_mark > 1.5, -1000.0, 0.0), (tile, LANES))
            best = None
            for a in range(b + 1):
                theirs = rows[k, a * src_tile : (a + 1) * src_tile].reshape(tile, width)
                similar = lax.dot_general(theirs, mine, contract, preferred_element_type=jnp.float32)
                if a == b:
                    similar = jnp.where(diagonal, -1000.0, similar)
                across = similar + col_bias
                across = jnp.maximum(across[:, :LANES], across[:, LANES:])
                down = similar + bias[a * tile : (a + 1) * tile, 0:1]
                down = jnp.max(down, axis=0, keepdims=True)
                if a == b:
                    row_best[a * tile : (a + 1) * tile, :] = across
                else:
                    row_best[a * tile : (a + 1) * tile, :] = jnp.maximum(row_best[a * tile : (a + 1) * tile, :], across)
                    best = down if best is None else jnp.maximum(best, down)
            if best is None:
                best = jnp.full((1, tile), -1.0, jnp.float32)
            col_best[:, b * tile : (b + 1) * tile] = jnp.maximum(best, -1.0)
        for b in range(blocks):
            across = jnp.max(row_best[b * tile : (b + 1) * tile, :].T, axis=0, keepdims=True)
            best = jnp.maximum(across, col_best[:, b * tile : (b + 1) * tile])
            for h in range(tile // LANES):
                q = b * (tile // LANES) + h
                packed[q : q + 1, :] = best[:, h * LANES : (h + 1) * LANES]
        group = LANES // MOST
        for g in range(group):
            out_ref[:, g, k * MOST : (k + 1) * MOST] = packed[:, g * MOST : (g + 1) * MOST]


def near(x, per):
    sources, pair, width = x.shape
    n = sources * MOST
    group = LANES // MOST
    return pl.pallas_call(
        near_kernel,
        out_shape=jax.ShapeDtypeStruct((sources // group, group, pair), jnp.float32),
        in_specs=[pl.BlockSpec(memory_space=pl.ANY)],
        out_specs=pl.BlockSpec(memory_space=pltpu.VMEM),
        scratch_shapes=[
            pltpu.VMEM((per, sources, MOST, width), jnp.bfloat16),
            pltpu.VMEM((n, LANES), jnp.float32),
            pltpu.VMEM((n, LANES), jnp.float32),
            pltpu.VMEM((1, n), jnp.float32),
            pltpu.VMEM((n // LANES, LANES), jnp.float32),
            pltpu.SemaphoreType.DMA((per, n // 256)),
        ],
        compiler_params=pltpu.CompilerParams(vmem_limit_bytes=48 * 1024 * 1024),
        name="near",
    )(x)


def pick_kernel(x_ref, target_ref, out_ref):
    owners, pair = x_ref.shape
    n = target_ref.shape[1]
    table = x_ref[...].T
    hi = table.astype(jnp.bfloat16)
    rest = table - hi.astype(jnp.float32)
    mid = rest.astype(jnp.bfloat16)
    low = (rest - mid.astype(jnp.float32)).astype(jnp.bfloat16)
    split = jnp.concatenate([hi, mid, low], axis=0)
    span = 512
    owner = lax.broadcasted_iota(jnp.int32, (owners, span), 0)
    slot = lax.broadcasted_iota(jnp.int32, (pair, span), 0)
    for b in range(n // span):
        target = target_ref[:, b * span : (b + 1) * span]
        hot = jnp.where(owner == target // pair, 1.0, 0.0).astype(jnp.bfloat16)
        got = jnp.dot(split, hot, preferred_element_type=jnp.float32)
        value = (got[:pair] + got[pair : 2 * pair]) + got[2 * pair :]
        out_ref[:, b * span : (b + 1) * span] = jnp.sum(
            jnp.where(slot == target % pair, value, 0.0), axis=0, keepdims=True
        )


def pick(x, target):
    return pl.pallas_call(
        pick_kernel,
        out_shape=jax.ShapeDtypeStruct(target.shape, jnp.float32),
        name="pick",
    )(x, target)


def per_device(embeddings, cluster_ids):
    n = embeddings.shape[0]
    axes = ("group", "blk")
    devices = lax.axis_size("group") * lax.axis_size("blk")
    per = CLUSTERS // devices
    outgoing, target = prep(embeddings, cluster_ids.reshape(1, n), CLUSTERS)
    outgoing = outgoing.reshape(devices, per * MOST, -1)
    members = lax.all_to_all(outgoing, axes, split_axis=0, concat_axis=0, tiled=True)
    best = near(members, per).reshape(devices, per * MOST)
    results = lax.all_to_all(best, axes, split_axis=0, concat_axis=0, tiled=True)
    return pick(results, target).reshape(n)


def solution(mesh):
    placed = (P(("group", "blk"), None), P(("group", "blk"), None))
    return jax.shard_map(
        per_device, mesh=mesh, in_specs=placed, out_specs=P(("group", "blk")), check_vma=False
    )
```

time: 263 us -> 154 us (0.59)
  other arithmetic: 37.4 us -> 0 us
  waiting for transfers between devices: 35.6 us -> 0 us
  local copies, waits for them, and re-layouts: 33 us -> 0.7 us
  Pallas kernels: 0 us -> 29 us
  matrix products: 24.3 us -> 0 us
  blocking collectives: 109 us -> 124 us
  between operations: 13.5 us -> 0.03 us
  starting transfers between devices: 10.1 us -> 0 us
    pallas_call x0 -> x3, Pallas kernels: none -> 29 us  [the longest x1 16.3 us: near(): pl.pallas_call(near_kernel, out_shape=jax.ShapeDtypeStruct((sources // gr...]
    dot_general x1 -> x0, matrix products: 24.3 us -> none  [per_device(): jnp.einsum('kpd,kqd->kpq', members, piece, preferred_element_type=jnp.flo...]
    all_gather x1 -> x0, waiting for transfers between devices: 23 us -> none  [per_device(): piece = lax.all_gather(members, 'blk', axis=1, tiled=True)]
    gather x1 -> x0, local copies, waits for them, and re-layouts: 20.5 us -> none  [per_device(): return results.reshape(-1)[target]]
    scatter x1 -> x0, other arithmetic: 15.8 us -> none  [per_device(): jnp.zeros((clusters * most, width), jnp.bfloat16).at[target].set(unit)]
    reduce_or x2 -> x0, other arithmetic: 15.2 us -> none  [the longest x1 7.83 us: per_device(): filled = jnp.any(members != 0, axis=-1)]
    all_to_all x1 -> x2, blocking collectives: 109 us -> 124 us  [the longest x1 110 us: per_device(): lax.all_to_all(outgoing, axes, split_axis=0, concat_axis=0, tiled=True)]
    all_to_all x1 -> x0, waiting for transfers between devices: 12.6 us -> none  [per_device(): lax.all_to_all(best[None], 'group', split_axis=2, concat_axis=0, tiled=True)]
  transfers between devices with their start and end apart: 2 -> 0, of which waited for: 2 -> 0; matrix products, arithmetic and copies ran while one was open for 4% -> 0% of each run, Pallas kernels for 0% -> 0%
where the time goes in v1:
time: 154 us
  blocking collectives  124 us (81%)
  Pallas kernels  29 us (19%)
    all_to_all x1, blocking collectives, per_device(): lax.all_to_all(outgoing, axes, split_axis=0, concat_axis=0, tiled=True)  110 us
    pallas_call x1, Pallas kernels, near(): pl.pallas_call(near_kernel, out_shape=jax.ShapeDtypeStruct((sources // gr...  16.3 us
    all_to_all x1, blocking collectives, per_device(): lax.all_to_all(best, axes, split_axis=0, concat_axis=0, tiled=True)  14.2 us
    pallas_call x1, Pallas kernels, prep(): pl.pallas_call(prep_kernel, out_shape=(jax.ShapeDtypeStruct((total, width...  11 us

profile of v1, /device:TPU:1, one launch (start us, length us, event | category | flops | bytes accessed | tf_op | source)
XLA Modules:
  0.0 153.5 jit_solution(11755060905778516815)
XLA Ops:
  0.0 0.0 copy-start
  0.0 0.7 copy-done
  0.7 11.0 %prep.1 = (bf16[4096,1024]{1,0:T(8,128)(2,1)}, s32[1,2048]{1,0:T(1,128)S(1)}) custom-call(bf16[2048,1024]{1,0:T(8,128)(2,1)} %x_hbm.1, s32[1,2048]{1,0:T(1,128)S(1)} %bitcast.8), custom_call_target="tpu_custom_call" | custom-call | tf_op jit(solution)/shard_map/prep/pallas_call | solution.py:105
  11.7 0.0 copy-start.1
  11.7 109.6 %all_to_all.16.x_hbm = bf16[128,32,1024]{2,1,0:T(8,128)(2,1)} all-to-all(bf16[128,32,1024]{2,1,0:T(8,128)(2,1)} %bitcast.9), channel_id=1, replica_groups=mesh['group'=64,'blk'=2] {'group','blk'}, dimensions={0} | all-to-all | bytes 16777216 | tf_op jit(solution)/shard_map/all_to_all | solution.py:249
  121.2 0.0 copy-done.1
  121.2 16.3 %near.1 = f32[16,8,32]{2,1,0:T(8,128)S(1)} custom-call(bf16[128,32,1024]{2,1,0:T(8,128)(2,1)} %all_to_all.16.x_hbm), custom_call_target="tpu_custom_call" | custom-call | tf_op jit(solution)/shard_map/near/pallas_call | solution.py:194
  137.5 14.2 %all_to_all.17 = f32[128,1,32]{2,1,0:T(1,128)} all-to-all(f32[128,1,32]{2,1,0:T(1,128)S(1)} %bitcast.7), channel_id=1, replica_groups=mesh['group'=64,'blk'=2] {'group','blk'}, dimensions={0} | all-to-all | bytes 32768 | tf_op jit(solution)/shard_map/all_to_all | solution.py:251
  151.8 1.8 %pick.1 = f32[1,2048]{1,0:T(1,128)} custom-call(f32[128,32]{1,0:T(8,128)} %bitcast.10, s32[1,2048]{1,0:T(1,128)} %copy-done.1), custom_call_target="tpu_custom_call" | custom-call | tf_op jit(solution)/shard_map/pick/pallas_call | solution.py:235
Async XLA Ops:
  0.0 0.7 copy-start
  11.7 109.6 %copy-start.1 = (s32[1,2048]{1,0:T(1,128)}, s32[1,2048]{1,0:T(1,128)S(1)}, u32[]{:S(2)}) copy-start(s32[1,2048]{1,0:T(1,128)S(1)} %get-tuple-element.8.target_ref) | copy-start | bytes 24580

commit v2 on v1

v2 whole, which is shorter than its diff:
```python
import jax
import jax.numpy as jnp
from jax import lax
from jax.experimental import pallas as pl
from jax.experimental.pallas import tpu as pltpu
from jax.sharding import PartitionSpec as P

CLUSTERS = 256
MOST = 16
LANES = 128
PAD = 2.0
FAR = -1000.0
PITCH = 9


def prep_kernel(
    x_hbm, label_hbm, out_hbm, target_ref, xbuf, label, at, rows, slots, obuf, where, in_sem, out_sem, small_sem
):
    n, width = x_hbm.shape
    chunks = width // LANES
    total = out_hbm.shape[0]
    clusters = total // MOST
    pitch = PITCH * chunks
    parts = in_sem.shape[0]
    step = n // parts
    fetch = pltpu.make_async_copy(label_hbm, label, small_sem.at[0])
    fetch.start()
    loads = [
        pltpu.make_async_copy(x_hbm.at[pl.ds(p * step, step)], xbuf.at[pl.ds(p * step, step)], in_sem.at[p])
        for p in range(parts)
    ]
    for load in loads:
        load.start()

    def fill(i, _):
        base = pl.multiple_of(i * 8 * pitch, 8 * pitch)
        slots[pl.ds(base, 8 * pitch), :] = jnp.full((8 * pitch, LANES), PAD, jnp.float32)
        return 0

    lax.fori_loop(0, total // 64, fill, 0)
    fetch.wait()
    span = 256
    before = (
        lax.broadcasted_iota(jnp.int32, (span, span), 0) < lax.broadcasted_iota(jnp.int32, (span, span), 1)
    ).astype(jnp.bfloat16)
    carry = jnp.zeros((clusters, 1), jnp.float32)
    cluster = lax.broadcasted_iota(jnp.int32, (clusters, span), 0)
    for b in range(n // span):
        name = label[:, b * span : (b + 1) * span]
        hit = cluster == name
        hot = jnp.where(hit, 1.0, 0.0)
        count = jnp.dot(hot.astype(jnp.bfloat16), before, preferred_element_type=jnp.float32) + carry
        rank = jnp.sum(jnp.where(hit, count, 0.0), axis=0, keepdims=True)
        carry = carry + jnp.sum(hot, axis=1, keepdims=True)
        target = name * MOST + rank.astype(jnp.int32)
        target_ref[:, b * span : (b + 1) * span] = target
        at[:, b * span : (b + 1) * span] = (target >> 3) * pitch + (target & 7)
    place = pltpu.make_async_copy(at, where, small_sem.at[1])
    place.start()

    for p in range(parts):
        loads[p].wait()

        def unit(i, _):
            r = pl.multiple_of(p * step + i * 16, 16)
            wide = xbuf[pl.ds(r, 16), :].astype(jnp.float32)
            scaled = wide * lax.rsqrt(jnp.sum(wide * wide, axis=1, keepdims=True) + 1e-06)
            base = (r >> 3) * pitch
            for h in range(2):
                for c in range(chunks):
                    rows[pl.ds(base + h * pitch + c * PITCH, 8), :] = scaled[
                        h * 8 : h * 8 + 8, c * LANES : (c + 1) * LANES
                    ]
            return 0

        lax.fori_loop(0, step // 16, unit, 0, unroll=step // 16)
    place.wait()
    batch = 64

    def move(i, _):
        got = [rows[pl.ds((i * (batch // 8) + u // 8) * pitch + u % 8, chunks, stride=PITCH), :] for u in range(batch)]
        for u in range(batch):
            slots[pl.ds(where[0, i * batch + u], chunks, stride=PITCH), :] = got[u]
        return 0

    lax.fori_loop(0, n // batch, move, 0, unroll=2)

    out_parts = out_sem.shape[0]
    out_step = total // out_parts
    stores = []
    for p in range(out_parts):

        def pack(i, _):
            r = pl.multiple_of(p * out_step + i * 16, 16)
            base = (r >> 3) * pitch
            low = [slots[pl.ds(base + c * PITCH, 8), :] for c in range(chunks)]
            high = [slots[pl.ds(base + pitch + c * PITCH, 8), :] for c in range(chunks)]
            both = [jnp.concatenate([a, b], axis=0).astype(jnp.bfloat16) for a, b in zip(low, high)]
            for c in range(chunks):
                obuf[pl.ds(r, 16), c * LANES : (c + 1) * LANES] = both[c]
            return 0

        lax.fori_loop(0, out_step // 16, pack, 0, unroll=8)
        store = pltpu.make_async_copy(
            obuf.at[pl.ds(p * out_step, out_step)], out_hbm.at[pl.ds(p * out_step, out_step)], out_sem.at[p]
        )
        store.start()
        stores.append(store)
    for store in stores:
        store.wait()


def prep(x, labels, clusters):
    n, width = x.shape
    total = clusters * MOST
    chunks = width // LANES
    return pl.pallas_call(
        prep_kernel,
        out_shape=(
            jax.ShapeDtypeStruct((total, width), jnp.bfloat16),
            jax.ShapeDtypeStruct((1, n), jnp.int32),
        ),
        in_specs=[pl.BlockSpec(memory_space=pl.ANY), pl.BlockSpec(memory_space=pltpu.HBM)],
        out_specs=(pl.BlockSpec(memory_space=pl.ANY), pl.BlockSpec(memory_space=pltpu.VMEM)),
        scratch_shapes=[
            pltpu.VMEM((n, width), jnp.bfloat16),
            pltpu.VMEM((1, n), jnp.int32),
            pltpu.VMEM((1, n), jnp.int32),
            pltpu.VMEM((n * PITCH // 8 * chunks, LANES), jnp.float32),
            pltpu.VMEM((total * PITCH // 8 * chunks, LANES), jnp.float32),
            pltpu.VMEM((total, width), jnp.bfloat16),
            pltpu.SMEM((1, n), jnp.int32),
            pltpu.SemaphoreType.DMA((4,)),
            pltpu.SemaphoreType.DMA((8,)),
            pltpu.SemaphoreType.DMA((2,)),
        ],
        compiler_params=pltpu.CompilerParams(vmem_limit_bytes=60 * 1024 * 1024),
        name="prep",
    )(x, labels)


def near_plan(per, blocks):
    cuts = [0] + [c for c in (1, 2, 4) if c < blocks] + [blocks]
    first = [(0, low, high) for low, high in zip(cuts[:-1], cuts[1:])]
    return first + [(k, 0, blocks) for k in range(1, per)]


def near_kernel(x_hbm, out_ref, rows, bias, row_best, col_best, packed, sem):
    sources, pair, width = x_hbm.shape
    per = pair // MOST
    tile = 256
    from_each = tile // MOST
    blocks = sources // from_each
    plan = near_plan(per, blocks)
    loads = [
        pltpu.make_async_copy(
            x_hbm.at[pl.ds(low * from_each, (high - low) * from_each), pl.ds(k * MOST, MOST), :],
            rows.at[k, pl.ds(low * from_each, (high - low) * from_each)],
            sem.at[i],
        )
        for i, (k, low, high) in enumerate(plan)
    ]
    for load in loads:
        load.start()
    contract = (((1,), (1,)), ((), ()))
    first = (lax.broadcasted_iota(jnp.int32, (8, LANES), 1) == 0).astype(jnp.bfloat16)
    diagonal = lax.broadcasted_iota(jnp.int32, (tile, tile), 0) == lax.broadcasted_iota(jnp.int32, (tile, tile), 1)

    def finish(k):
        for b in range(blocks):
            across = jnp.max(row_best[k, b * tile : (b + 1) * tile, :].T, axis=0, keepdims=True)
            best = jnp.maximum(across, col_best[k : k + 1, b * tile : (b + 1) * tile])
            for h in range(tile // LANES):
                q = b * (tile // LANES) + h
                packed[k, q : q + 1, :] = best[:, h * LANES : (h + 1) * LANES]
        for g in range(LANES // MOST):
            out_ref[:, g, k * MOST : (k + 1) * MOST] = packed[k, :, g * MOST : (g + 1) * MOST]

    for i, (k, low, high) in enumerate(plan):
        loads[i].wait()
        if k > 0 and low == 0:
            finish(k - 1)
        for b in range(low, high):
            mine = rows[k, b * from_each : (b + 1) * from_each].reshape(tile, width)
            row_mark = mine[:, 0:1].astype(jnp.float32)
            bias[k, b * tile : (b + 1) * tile, :] = jnp.broadcast_to(jnp.where(row_mark > 1.5, FAR, 0.0), (tile, LANES))
            col_mark = lax.dot_general(first, mine[:, :LANES], contract, preferred_element_type=jnp.float32)[0:1]
            col_bias = jnp.where(col_mark > 1.5, FAR, 0.0)
            best = jnp.full((8, tile), -1.0, jnp.float32)
            for a in [b] + list(range(b)):
                theirs = rows[k, a * from_each : (a + 1) * from_each].reshape(tile, width)
                similar = lax.dot_general(theirs, mine, contract, preferred_element_type=jnp.float32)
                if a == b:
                    similar = jnp.where(diagonal, FAR, similar)
                across = similar + col_bias
                across = jnp.maximum(across[:, :LANES], across[:, LANES:])
                if a == b:
                    row_best[k, a * tile : (a + 1) * tile, :] = across
                else:
                    row_best[k, a * tile : (a + 1) * tile, :] = jnp.maximum(
                        row_best[k, a * tile : (a + 1) * tile, :], across
                    )
                    down = similar + bias[k, a * tile : (a + 1) * tile, 0:1]
                    best = jnp.maximum(best, jnp.max(down.reshape(tile // 8, 8, tile), axis=0))
            col_best[k : k + 1, b * tile : (b + 1) * tile] = jnp.max(best, axis=0, keepdims=True)
    finish(per - 1)


def near(x, per):
    sources, pair, width = x.shape
    n = sources * MOST
    group = LANES // MOST
    return pl.pallas_call(
        near_kernel,
        out_shape=jax.ShapeDtypeStruct((sources // group, group, pair), jnp.float32),
        in_specs=[pl.BlockSpec(memory_space=pl.ANY)],
        out_specs=pl.BlockSpec(memory_space=pltpu.VMEM),
        scratch_shapes=[
            pltpu.VMEM((per, sources, MOST, width), jnp.bfloat16),
            pltpu.VMEM((per, n, LANES), jnp.float32),
            pltpu.VMEM((per, n, LANES), jnp.float32),
            pltpu.VMEM((per, n), jnp.float32),
            pltpu.VMEM((per, n // LANES, LANES), jnp.float32),
            pltpu.SemaphoreType.DMA((len(near_plan(per, n // 256)),)),
        ],
        compiler_params=pltpu.CompilerParams(vmem_limit_bytes=48 * 1024 * 1024),
        name="near",
    )(x)


def pick_kernel(x_ref, target_ref, out_ref):
    owners, pair = x_ref.shape
    n = target_ref.shape[1]
    table = x_ref[...].T
    hi = table.astype(jnp.bfloat16)
    rest = table - hi.astype(jnp.float32)
    mid = rest.astype(jnp.bfloat16)
    low = (rest - mid.astype(jnp.float32)).astype(jnp.bfloat16)
    split = jnp.concatenate([hi, mid, low], axis=0)
    span = 512
    owner = lax.broadcasted_iota(jnp.int32, (owners, span), 0)
    slot = lax.broadcasted_iota(jnp.int32, (pair, span), 0)
    for b in range(n // span):
        target = target_ref[:, b * span : (b + 1) * span]
        hot = jnp.where(owner == target // pair, 1.0, 0.0).astype(jnp.bfloat16)
        got = jnp.dot(split, hot, preferred_element_type=jnp.float32)
        value = (got[:pair] + got[pair : 2 * pair]) + got[2 * pair :]
        out_ref[:, b * span : (b + 1) * span] = jnp.sum(
            jnp.where(slot == target % pair, value, 0.0), axis=0, keepdims=True
        )


def pick(x, target):
    return pl.pallas_call(
        pick_kernel,
        out_shape=jax.ShapeDtypeStruct(target.shape, jnp.float32),
        name="pick",
    )(x, target)


def per_device(embeddings, cluster_ids):
    n = embeddings.shape[0]
    axes = ("group", "blk")
    devices = lax.axis_size("group") * lax.axis_size("blk")
    per = CLUSTERS // devices
    outgoing, target = prep(embeddings, cluster_ids.reshape(1, n), CLUSTERS)
    outgoing = outgoing.reshape(devices, per * MOST, -1)
    members = lax.all_to_all(outgoing, axes, split_axis=0, concat_axis=0, tiled=True)
    best = near(members, per).reshape(devices, per * MOST)
    results = lax.all_to_all(best, axes, split_axis=0, concat_axis=0, tiled=True)
    return pick(results, target).reshape(n)


def solution(mesh):
    placed = (P(("group", "blk"), None), P(("group", "blk"), None))
    return jax.shard_map(
        per_device, mesh=mesh, in_specs=placed, out_specs=P(("group", "blk")), check_vma=False
    )
```

time: 154 us -> 149 us (0.968)
  Pallas kernels: 29 us -> 24.4 us
    pallas_call x1, Pallas kernels: 16.3 us -> 13 us  [near(): pl.pallas_call(near_kernel, out_shape=jax.ShapeDtypeStruct((sources // gr...]
where the time goes in v2:
time: 149 us; the launch traced here: 148 us
  blocking collectives  124 us (83%)
  Pallas kernels  24.4 us (16%)
    all_to_all x1, blocking collectives, per_device(): lax.all_to_all(outgoing, axes, split_axis=0, concat_axis=0, tiled=True)  110 us
    all_to_all x1, blocking collectives, per_device(): lax.all_to_all(best, axes, split_axis=0, concat_axis=0, tiled=True)  14.3 us
    pallas_call x1, Pallas kernels, near(): pl.pallas_call(near_kernel, out_shape=jax.ShapeDtypeStruct((sources // gr...  13 us
    pallas_call x1, Pallas kernels, prep(): pl.pallas_call(prep_kernel, out_shape=(jax.ShapeDtypeStruct((total, width...  9.61 us

profile of v2, /device:TPU:1, one launch (start us, length us, event | category | flops | bytes accessed | tf_op | source)
XLA Modules:
  0.0 148.3 jit_solution(1441682029741840280)
XLA Ops:
  0.0 9.6 %prep.1 = (bf16[4096,1024]{1,0:T(8,128)(2,1)}, s32[1,2048]{1,0:T(1,128)}) custom-call(bf16[2048,1024]{1,0:T(8,128)(2,1)} %x_hbm.1, s32[1,2048]{1,0:T(1,128)} %bitcast.10), custom_call_target="tpu_custom_call" | custom-call | tf_op jit(solution)/shard_map/prep/pallas_call | solution.py:117
  9.6 109.6 %all_to_all.16.x_hbm = bf16[128,32,1024]{2,1,0:T(8,128)(2,1)} all-to-all(bf16[128,32,1024]{2,1,0:T(8,128)(2,1)} %bitcast.8), channel_id=1, replica_groups=mesh['group'=64,'blk'=2] {'group','blk'}, dimensions={0} | all-to-all | bytes 16777216 | tf_op jit(solution)/shard_map/all_to_all | solution.py:268
  119.2 13.0 %near.1 = f32[16,8,32]{2,1,0:T(8,128)S(1)} custom-call(bf16[128,32,1024]{2,1,0:T(8,128)(2,1)} %all_to_all.16.x_hbm), custom_call_target="tpu_custom_call" | custom-call | tf_op jit(solution)/shard_map/near/pallas_call | solution.py:213
  132.2 14.3 %all_to_all.17 = f32[128,1,32]{2,1,0:T(1,128)} all-to-all(f32[128,1,32]{2,1,0:T(1,128)S(1)} %bitcast.7), channel_id=1, replica_groups=mesh['group'=64,'blk'=2] {'group','blk'}, dimensions={0} | all-to-all | bytes 32768 | tf_op jit(solution)/shard_map/all_to_all | solution.py:270
  146.5 1.8 %pick.1 = f32[1,2048]{1,0:T(1,128)} custom-call(f32[128,32]{1,0:T(8,128)} %bitcast.9, s32[1,2048]{1,0:T(1,128)} %get-tuple-element.8.target_ref), custom_call_target="tpu_custom_call" | custom-call | tf_op jit(solution)/shard_map/pick/pallas_call | solution.py:254

commit v3 on v2

--- a/solution.py
+++ b/solution.py
@@ -61,21 +61,15 @@
     for p in range(parts):
         loads[p].wait()
 
-        def unit(i, _):
-            r = pl.multiple_of(p * step + i * 16, 16)
-            wide = xbuf[pl.ds(r, 16), :].astype(jnp.float32)
+        for r in range(p * step, (p + 1) * step, 16):
+            wide = xbuf[r : r + 16, :].astype(jnp.float32)
             scaled = wide * lax.rsqrt(jnp.sum(wide * wide, axis=1, keepdims=True) + 1e-06)
-            base = (r >> 3) * pitch
             for h in range(2):
                 for c in range(chunks):
-                    rows[pl.ds(base + h * pitch + c * PITCH, 8), :] = scaled[
-                        h * 8 : h * 8 + 8, c * LANES : (c + 1) * LANES
-                    ]
-            return 0
-
-        lax.fori_loop(0, step // 16, unit, 0, unroll=step // 16)
+                    low = (r // 8 + h) * pitch + c * PITCH
+                    rows[low : low + 8, :] = scaled[h * 8 : h * 8 + 8, c * LANES : (c + 1) * LANES]
     place.wait()
-    batch = 64
+    batch = 16
 
     def move(i, _):
         got = [rows[pl.ds((i * (batch // 8) + u // 8) * pitch + u % 8, chunks, stride=PITCH), :] for u in range(batch)]
@@ -83,7 +77,7 @@
             slots[pl.ds(where[0, i * batch + u], chunks, stride=PITCH), :] = got[u]
         return 0
 
-    lax.fori_loop(0, n // batch, move, 0, unroll=2)
+    lax.fori_loop(0, n // batch, move, 0, unroll=n // batch)
 
     out_parts = out_sem.shape[0]
     out_step = total // out_parts
@@ -100,7 +94,7 @@
                 obuf[pl.ds(r, 16), c * LANES : (c + 1) * LANES] = both[c]
             return 0
 
-        lax.fori_loop(0, out_step // 16, pack, 0, unroll=8)
+        lax.fori_loop(0, out_step // 16, pack, 0, unroll=out_step // 16)
         store = pltpu.make_async_copy(
             obuf.at[pl.ds(p * out_step, out_step)], out_hbm.at[pl.ds(p * out_step, out_step)], out_sem.at[p]
         )
@@ -237,16 +231,17 @@
     mid = rest.astype(jnp.bfloat16)
     low = (rest - mid.astype(jnp.float32)).astype(jnp.bfloat16)
     split = jnp.concatenate([hi, mid, low], axis=0)
-    span = 512
+    shift = pair.bit_length() - 1
+    span = 1024
     owner = lax.broadcasted_iota(jnp.int32, (owners, span), 0)
     slot = lax.broadcasted_iota(jnp.int32, (pair, span), 0)
     for b in range(n // span):
         target = target_ref[:, b * span : (b + 1) * span]
-        hot = jnp.where(owner == target // pair, 1.0, 0.0).astype(jnp.bfloat16)
+        hot = jnp.where(owner == target >> shift, 1.0, 0.0).astype(jnp.bfloat16)
         got = jnp.dot(split, hot, preferred_element_type=jnp.float32)
         value = (got[:pair] + got[pair : 2 * pair]) + got[2 * pair :]
         out_ref[:, b * span : (b + 1) * span] = jnp.sum(
-            jnp.where(slot == target % pair, value, 0.0), axis=0, keepdims=True
+            jnp.where(slot == (target & (pair - 1)), value, 0.0), axis=0, keepdims=True
         )
 
 

time: 149 us -> 148 us (level)
  no operation moved by 1% of the time
where the time goes in v3:
time: 148 us
  blocking collectives  124 us (84%)
  Pallas kernels  23.7 us (16%)
    all_to_all x1, blocking collectives, per_device(): lax.all_to_all(outgoing, axes, split_axis=0, concat_axis=0, tiled=True)  110 us
    all_to_all x1, blocking collectives, per_device(): lax.all_to_all(best, axes, split_axis=0, concat_axis=0, tiled=True)  14.3 us
    pallas_call x1, Pallas kernels, near(): pl.pallas_call(near_kernel, out_shape=jax.ShapeDtypeStruct((sources // gr...  13 us
    pallas_call x1, Pallas kernels, prep(): pl.pallas_call(prep_kernel, out_shape=(jax.ShapeDtypeStruct((total, width...  8.92 us

profile of v3, /device:TPU:1, one launch (start us, length us, event | category | flops | bytes accessed | tf_op | source)
XLA Modules:
  0.0 147.6 jit_solution(116883464961574715)
XLA Ops:
  0.0 8.9 %prep.1 = (bf16[4096,1024]{1,0:T(8,128)(2,1)}, s32[1,2048]{1,0:T(1,128)}) custom-call(bf16[2048,1024]{1,0:T(8,128)(2,1)} %x_hbm.1, s32[1,2048]{1,0:T(1,128)} %bitcast.10), custom_call_target="tpu_custom_call" | custom-call | tf_op jit(solution)/shard_map/prep/pallas_call | solution.py:111
  8.9 109.6 %all_to_all.16.x_hbm = bf16[128,32,1024]{2,1,0:T(8,128)(2,1)} all-to-all(bf16[128,32,1024]{2,1,0:T(8,128)(2,1)} %bitcast.8), channel_id=1, replica_groups=mesh['group'=64,'blk'=2] {'group','blk'}, dimensions={0} | all-to-all | bytes 16777216 | tf_op jit(solution)/shard_map/all_to_all | solution.py:263
  118.5 13.0 %near.1 = f32[16,8,32]{2,1,0:T(8,128)S(1)} custom-call(bf16[128,32,1024]{2,1,0:T(8,128)(2,1)} %all_to_all.16.x_hbm), custom_call_target="tpu_custom_call" | custom-call | tf_op jit(solution)/shard_map/near/pallas_call | solution.py:207
  131.5 14.3 %all_to_all.17 = f32[128,1,32]{2,1,0:T(1,128)} all-to-all(f32[128,1,32]{2,1,0:T(1,128)S(1)} %bitcast.7), channel_id=1, replica_groups=mesh['group'=64,'blk'=2] {'group','blk'}, dimensions={0} | all-to-all | bytes 32768 | tf_op jit(solution)/shard_map/all_to_all | solution.py:265
  145.8 1.8 %pick.1 = f32[1,2048]{1,0:T(1,128)} custom-call(f32[128,32]{1,0:T(8,128)} %bitcast.9, s32[1,2048]{1,0:T(1,128)} %get-tuple-element.8.target_ref), custom_call_target="tpu_custom_call" | custom-call | tf_op jit(solution)/shard_map/pick/pallas_call | solution.py:249

commit v4 on v3

--- a/solution.py
+++ b/solution.py
@@ -133,57 +133,29 @@
     )(x, labels)
 
 
-def near_plan(per, blocks):
-    cuts = [0] + [c for c in (1, 2, 4) if c < blocks] + [blocks]
-    first = [(0, low, high) for low, high in zip(cuts[:-1], cuts[1:])]
-    return first + [(k, 0, blocks) for k in range(1, per)]
-
-
-def near_kernel(x_hbm, out_ref, rows, bias, row_best, col_best, packed, sem):
-    sources, pair, width = x_hbm.shape
+def near_kernel(x_ref, out_ref, bias, row_best, col_best, packed):
+    sources, pair, width = x_ref.shape
     per = pair // MOST
     tile = 256
     from_each = tile // MOST
     blocks = sources // from_each
-    plan = near_plan(per, blocks)
-    loads = [
-        pltpu.make_async_copy(
-            x_hbm.at[pl.ds(low * from_each, (high - low) * from_each), pl.ds(k * MOST, MOST), :],
-            rows.at[k, pl.ds(low * from_each, (high - low) * from_each)],
-            sem.at[i],
-        )
-        for i, (k, low, high) in enumerate(plan)
-    ]
-    for load in loads:
-        load.start()
     contract = (((1,), (1,)), ((), ()))
     first = (lax.broadcasted_iota(jnp.int32, (8, LANES), 1) == 0).astype(jnp.bfloat16)
     diagonal = lax.broadcasted_iota(jnp.int32, (tile, tile), 0) == lax.broadcasted_iota(jnp.int32, (tile, tile), 1)
 
-    def finish(k):
+    def members(k, b):
+        return x_ref[b * from_each : (b + 1) * from_each, k * MOST : (k + 1) * MOST, :].reshape(tile, width)
+
+    for k in range(per):
         for b in range(blocks):
-            across = jnp.max(row_best[k, b * tile : (b + 1) * tile, :].T, axis=0, keepdims=True)
-            best = jnp.maximum(across, col_best[k : k + 1, b * tile : (b + 1) * tile])
-            for h in range(tile // LANES):
-                q = b * (tile // LANES) + h
-                packed[k, q : q + 1, :] = best[:, h * LANES : (h + 1) * LANES]
-        for g in range(LANES // MOST):
-            out_ref[:, g, k * MOST : (k + 1) * MOST] = packed[k, :, g * MOST : (g + 1) * MOST]
-
-    for i, (k, low, high) in enumerate(plan):
-        loads[i].wait()
-        if k > 0 and low == 0:
-            finish(k - 1)
-        for b in range(low, high):
-            mine = rows[k, b * from_each : (b + 1) * from_each].reshape(tile, width)
+            mine = members(k, b)
             row_mark = mine[:, 0:1].astype(jnp.float32)
             bias[k, b * tile : (b + 1) * tile, :] = jnp.broadcast_to(jnp.where(row_mark > 1.5, FAR, 0.0), (tile, LANES))
             col_mark = lax.dot_general(first, mine[:, :LANES], contract, preferred_element_type=jnp.float32)[0:1]
             col_bias = jnp.where(col_mark > 1.5, FAR, 0.0)
             best = jnp.full((8, tile), -1.0, jnp.float32)
             for a in [b] + list(range(b)):
-                theirs = rows[k, a * from_each : (a + 1) * from_each].reshape(tile, width)
-                similar = lax.dot_general(theirs, mine, contract, preferred_element_type=jnp.float32)
+                similar = lax.dot_general(members(k, a), mine, contract, preferred_element_type=jnp.float32)
                 if a == b:
                     similar = jnp.where(diagonal, FAR, similar)
                 across = similar + col_bias
@@ -197,7 +169,14 @@
                     down = similar + bias[k, a * tile : (a + 1) * tile, 0:1]
                     best = jnp.maximum(best, jnp.max(down.reshape(tile // 8, 8, tile), axis=0))
             col_best[k : k + 1, b * tile : (b + 1) * tile] = jnp.max(best, axis=0, keepdims=True)
-    finish(per - 1)
+        for b in range(blocks):
+            across = jnp.max(row_best[k, b * tile : (b + 1) * tile, :].T, axis=0, keepdims=True)
+            best = jnp.maximum(across, col_best[k : k + 1, b * tile : (b + 1) * tile])
+            for h in range(tile // LANES):
+                q = b * (tile // LANES) + h
+                packed[k, q : q + 1, :] = best[:, h * LANES : (h + 1) * LANES]
+        for g in range(LANES // MOST):
+            out_ref[:, g, k * MOST : (k + 1) * MOST] = packed[k, :, g * MOST : (g + 1) * MOST]
 
 
 def near(x, per):
@@ -207,17 +186,15 @@
     return pl.pallas_call(
         near_kernel,
         out_shape=jax.ShapeDtypeStruct((sources // group, group, pair), jnp.float32),
-        in_specs=[pl.BlockSpec(memory_space=pl.ANY)],
+        in_specs=[pl.BlockSpec(memory_space=pltpu.VMEM)],
         out_specs=pl.BlockSpec(memory_space=pltpu.VMEM),
         scratch_shapes=[
-            pltpu.VMEM((per, sources, MOST, width), jnp.bfloat16),
             pltpu.VMEM((per, n, LANES), jnp.float32),
             pltpu.VMEM((per, n, LANES), jnp.float32),
             pltpu.VMEM((per, n), jnp.float32),
             pltpu.VMEM((per, n // LANES, LANES), jnp.float32),
-            pltpu.SemaphoreType.DMA((len(near_plan(per, n // 256)),)),
         ],
-        compiler_params=pltpu.CompilerParams(vmem_limit_bytes=48 * 1024 * 1024),
+        compiler_params=pltpu.CompilerParams(vmem_limit_bytes=16 * 1024 * 1024),
         name="near",
     )(x)
 

time: 148 us -> 146 us (0.986)
  Pallas kernels: 23.7 us -> 21.7 us
    pallas_call x1, Pallas kernels: 13 us -> 11 us  [near(): pl.pallas_call(near_kernel, out_shape=jax.ShapeDtypeStruct((sources // gr...]
where the time goes in v4:
time: 146 us; the launch traced here: 145 us
  blocking collectives  124 us (85%)
  Pallas kernels  21.7 us (15%)
    all_to_all x1, blocking collectives, per_device(): lax.all_to_all(outgoing, axes, split_axis=0, concat_axis=0, tiled=True)  109 us
    all_to_all x1, blocking collectives, per_device(): lax.all_to_all(best, axes, split_axis=0, concat_axis=0, tiled=True)  14.3 us
    pallas_call x1, Pallas kernels, near(): pl.pallas_call(near_kernel, out_shape=jax.ShapeDtypeStruct((sources // gr...  11 us
    pallas_call x1, Pallas kernels, prep(): pl.pallas_call(prep_kernel, out_shape=(jax.ShapeDtypeStruct((total, width...  8.91 us

profile of v4, /device:TPU:1, one launch (start us, length us, event | category | flops | bytes accessed | tf_op | source)
XLA Modules:
  0.0 145.4 jit_solution(15439044115782733662)
XLA Ops:
  0.0 8.9 %prep.1 = (bf16[4096,1024]{1,0:T(8,128)(2,1)}, s32[1,2048]{1,0:T(1,128)}) custom-call(bf16[2048,1024]{1,0:T(8,128)(2,1)} %x_hbm.1, s32[1,2048]{1,0:T(1,128)} %bitcast.10), custom_call_target="tpu_custom_call" | custom-call | tf_op jit(solution)/shard_map/prep/pallas_call | solution.py:111
  8.9 109.4 %all_to_all.16.x_ref = bf16[128,32,1024]{2,1,0:T(8,128)(2,1)S(1)} all-to-all(bf16[128,32,1024]{2,1,0:T(8,128)(2,1)} %bitcast.8), channel_id=1, replica_groups=mesh['group'=64,'blk'=2] {'group','blk'}, dimensions={0} | all-to-all | bytes 16777216 | tf_op jit(solution)/shard_map/all_to_all | solution.py:240
  118.4 11.0 %near.1 = f32[16,8,32]{2,1,0:T(8,128)S(1)} custom-call(bf16[128,32,1024]{2,1,0:T(8,128)(2,1)S(1)} %all_to_all.16.x_ref), custom_call_target="tpu_custom_call" | custom-call | tf_op jit(solution)/shard_map/near/pallas_call | solution.py:186
  129.4 14.3 %all_to_all.17 = f32[128,1,32]{2,1,0:T(1,128)} all-to-all(f32[128,1,32]{2,1,0:T(1,128)S(1)} %bitcast.7), channel_id=1, replica_groups=mesh['group'=64,'blk'=2] {'group','blk'}, dimensions={0} | all-to-all | bytes 32768 | tf_op jit(solution)/shard_map/all_to_all | solution.py:242
  143.7 1.8 %pick.1 = f32[1,2048]{1,0:T(1,128)} custom-call(f32[128,32]{1,0:T(8,128)} %bitcast.9, s32[1,2048]{1,0:T(1,128)} %get-tuple-element.8.target_ref), custom_call_target="tpu_custom_call" | custom-call | tf_op jit(solution)/shard_map/pick/pallas_call | solution.py:226

commit v5 on v4

--- a/solution.py
+++ b/solution.py
@@ -14,11 +14,11 @@
 
 
 def prep_kernel(
-    x_hbm, label_hbm, out_hbm, target_ref, xbuf, label, at, rows, slots, obuf, where, in_sem, out_sem, small_sem
+    x_hbm, label_hbm, out_ref, target_ref, xbuf, label, at, rows, slots, where, in_sem, small_sem
 ):
     n, width = x_hbm.shape
     chunks = width // LANES
-    total = out_hbm.shape[0]
+    total = out_ref.shape[0]
     clusters = total // MOST
     pitch = PITCH * chunks
     parts = in_sem.shape[0]
@@ -79,29 +79,13 @@
 
     lax.fori_loop(0, n // batch, move, 0, unroll=n // batch)
 
-    out_parts = out_sem.shape[0]
-    out_step = total // out_parts
-    stores = []
-    for p in range(out_parts):
-
-        def pack(i, _):
-            r = pl.multiple_of(p * out_step + i * 16, 16)
-            base = (r >> 3) * pitch
-            low = [slots[pl.ds(base + c * PITCH, 8), :] for c in range(chunks)]
-            high = [slots[pl.ds(base + pitch + c * PITCH, 8), :] for c in range(chunks)]
-            both = [jnp.concatenate([a, b], axis=0).astype(jnp.bfloat16) for a, b in zip(low, high)]
-            for c in range(chunks):
-                obuf[pl.ds(r, 16), c * LANES : (c + 1) * LANES] = both[c]
-            return 0
-
-        lax.fori_loop(0, out_step // 16, pack, 0, unroll=out_step // 16)
-        store = pltpu.make_async_copy(
-            obuf.at[pl.ds(p * out_step, out_step)], out_hbm.at[pl.ds(p * out_step, out_step)], out_sem.at[p]
-        )
-        store.start()
-        stores.append(store)
-    for store in stores:
-        store.wait()
+    for r in range(0, total, 16):
+        base = r // 8 * pitch
+        low = [slots[base + c * PITCH : base + c * PITCH + 8, :] for c in range(chunks)]
+        high = [slots[base + pitch + c * PITCH : base + pitch + c * PITCH + 8, :] for c in range(chunks)]
+        both = [jnp.concatenate([a, b], axis=0).astype(jnp.bfloat16) for a, b in zip(low, high)]
+        for c in range(chunks):
+            out_ref[r : r + 16, c * LANES : (c + 1) * LANES] = both[c]
 
 
 def prep(x, labels, clusters):
@@ -115,20 +99,18 @@
             jax.ShapeDtypeStruct((1, n), jnp.int32),
         ),
         in_specs=[pl.BlockSpec(memory_space=pl.ANY), pl.BlockSpec(memory_space=pltpu.HBM)],
-        out_specs=(pl.BlockSpec(memory_space=pl.ANY), pl.BlockSpec(memory_space=pltpu.VMEM)),
+        out_specs=(pl.BlockSpec(memory_space=pltpu.VMEM), pl.BlockSpec(memory_space=pltpu.VMEM)),
         scratch_shapes=[
             pltpu.VMEM((n, width), jnp.bfloat16),
             pltpu.VMEM((1, n), jnp.int32),
             pltpu.VMEM((1, n), jnp.int32),
             pltpu.VMEM((n * PITCH // 8 * chunks, LANES), jnp.float32),
             pltpu.VMEM((total * PITCH // 8 * chunks, LANES), jnp.float32),
-            pltpu.VMEM((total, width), jnp.bfloat16),
             pltpu.SMEM((1, n), jnp.int32),
             pltpu.SemaphoreType.DMA((4,)),
-            pltpu.SemaphoreType.DMA((8,)),
             pltpu.SemaphoreType.DMA((2,)),
         ],
-        compiler_params=pltpu.CompilerParams(vmem_limit_bytes=60 * 1024 * 1024),
+        compiler_params=pltpu.CompilerParams(vmem_limit_bytes=44 * 1024 * 1024),
         name="prep",
     )(x, labels)
 
@@ -235,7 +217,9 @@
     axes = ("group", "blk")
     devices = lax.axis_size("group") * lax.axis_size("blk")
     per = CLUSTERS // devices
-    outgoing, target = prep(embeddings, cluster_ids.reshape(1, n), CLUSTERS)
+    rows = pltpu.with_memory_space_constraint(embeddings, pltpu.HBM)
+    labels = pltpu.with_memory_space_constraint(cluster_ids.reshape(1, n), pltpu.HBM)
+    outgoing, target = prep(rows, labels, CLUSTERS)
     outgoing = outgoing.reshape(devices, per * MOST, -1)
     members = lax.all_to_all(outgoing, axes, split_axis=0, concat_axis=0, tiled=True)
     best = near(members, per).reshape(devices, per * MOST)

time: 146 us -> 142 us (0.973)
  Pallas kernels: 21.7 us -> 18.5 us
    pallas_call x1, Pallas kernels: 8.91 us -> 5.77 us  [prep(): pl.pallas_call(prep_kernel, out_shape=(jax.ShapeDtypeStruct((total, width...]
where the time goes in v5:
time: 142 us
  blocking collectives  123 us (87%)
  Pallas kernels  18.5 us (13%)
    all_to_all x1, blocking collectives, per_device(): lax.all_to_all(outgoing, axes, split_axis=0, concat_axis=0, tiled=True)  109 us
    all_to_all x1, blocking collectives, per_device(): lax.all_to_all(best, axes, split_axis=0, concat_axis=0, tiled=True)  14.2 us
    pallas_call x1, Pallas kernels, near(): pl.pallas_call(near_kernel, out_shape=jax.ShapeDtypeStruct((sources // gr...  11 us
    pallas_call x1, Pallas kernels, prep(): pl.pallas_call(prep_kernel, out_shape=(jax.ShapeDtypeStruct((total, width...  5.77 us

profile of v5, /device:TPU:1, one launch (start us, length us, event | category | flops | bytes accessed | tf_op | source)
XLA Modules:
  0.0 142.0 jit_solution(1756975391213463930)
XLA Ops:
  0.0 5.8 %prep.1 = (bf16[4096,1024]{1,0:T(8,128)(2,1)S(1)}, s32[1,2048]{1,0:T(1,128)S(1)}) custom-call(bf16[2048,1024]{1,0:T(8,128)(2,1)} %x_hbm.1, s32[1,2048]{1,0:T(1,128)} %bitcast.10), custom_call_target="tpu_custom_call" | custom-call | tf_op jit(solution)/shard_map/prep/pallas_call | solution.py:95
  5.8 0.0 copy-start
  5.8 109.2 %all_to_all.16.x_ref = bf16[128,32,1024]{2,1,0:T(8,128)(2,1)S(1)} all-to-all(bf16[128,32,1024]{2,1,0:T(8,128)(2,1)S(1)} %bitcast.7), channel_id=1, replica_groups=mesh['group'=64,'blk'=2] {'group','blk'}, dimensions={0} | all-to-all | bytes 16777216 | tf_op jit(solution)/shard_map/all_to_all | solution.py:224
  115.0 0.0 copy-done
  115.0 11.0 %near.1 = f32[16,8,32]{2,1,0:T(8,128)S(1)} custom-call(bf16[128,32,1024]{2,1,0:T(8,128)(2,1)S(1)} %all_to_all.16.x_ref), custom_call_target="tpu_custom_call" | custom-call | tf_op jit(solution)/shard_map/near/pallas_call | solution.py:168
  126.0 14.2 %all_to_all.17 = f32[128,1,32]{2,1,0:T(1,128)} all-to-all(f32[128,1,32]{2,1,0:T(1,128)S(1)} %bitcast.8), channel_id=1, replica_groups=mesh['group'=64,'blk'=2] {'group','blk'}, dimensions={0} | all-to-all | bytes 32768 | tf_op jit(solution)/shard_map/all_to_all | solution.py:226
  140.2 1.8 %pick.1 = f32[1,2048]{1,0:T(1,128)} custom-call(f32[128,32]{1,0:T(8,128)} %bitcast.9, s32[1,2048]{1,0:T(1,128)} %copy-done), custom_call_target="tpu_custom_call" | custom-call | tf_op jit(solution)/shard_map/pick/pallas_call | solution.py:208
Async XLA Ops:
  5.8 109.3 %copy-start = (s32[1,2048]{1,0:T(1,128)}, s32[1,2048]{1,0:T(1,128)S(1)}, u32[]{:S(2)}) copy-start(s32[1,2048]{1,0:T(1,128)S(1)} %get-tuple-element.8.target_ref) | copy-start | bytes 24580

commit v6 on v5

--- a/solution.py
+++ b/solution.py
@@ -104,8 +104,8 @@
             pltpu.VMEM((n, width), jnp.bfloat16),
             pltpu.VMEM((1, n), jnp.int32),
             pltpu.VMEM((1, n), jnp.int32),
-            pltpu.VMEM((n * PITCH // 8 * chunks, LANES), jnp.float32),
-            pltpu.VMEM((total * PITCH // 8 * chunks, LANES), jnp.float32),
+            pltpu.VMEM(((n // 8 + 1) * PITCH * chunks, LANES), jnp.float32),
+            pltpu.VMEM(((total // 8 + 1) * PITCH * chunks, LANES), jnp.float32),
             pltpu.SMEM((1, n), jnp.int32),
             pltpu.SemaphoreType.DMA((4,)),
             pltpu.SemaphoreType.DMA((2,)),

time: 142 us -> 142 us (level)
  no operation moved by 1% of the time
where the time goes in v6:
time: 142 us
  blocking collectives  123 us (87%)
  Pallas kernels  18.5 us (13%)
    all_to_all x1, blocking collectives, per_device(): lax.all_to_all(outgoing, axes, split_axis=0, concat_axis=0, tiled=True)  109 us
    all_to_all x1, blocking collectives, per_device(): lax.all_to_all(best, axes, split_axis=0, concat_axis=0, tiled=True)  14.2 us
    pallas_call x1, Pallas kernels, near(): pl.pallas_call(near_kernel, out_shape=jax.ShapeDtypeStruct((sources // gr...  11 us
    pallas_call x1, Pallas kernels, prep(): pl.pallas_call(prep_kernel, out_shape=(jax.ShapeDtypeStruct((total, width...  5.77 us

profile of v6, /device:TPU:1, one launch (start us, length us, event | category | flops | bytes accessed | tf_op | source)
XLA Modules:
  0.0 142.0 jit_solution(16227360901181053355)
XLA Ops:
  0.0 5.8 %prep.1 = (bf16[4096,1024]{1,0:T(8,128)(2,1)S(1)}, s32[1,2048]{1,0:T(1,128)S(1)}) custom-call(bf16[2048,1024]{1,0:T(8,128)(2,1)} %x_hbm.1, s32[1,2048]{1,0:T(1,128)} %bitcast.10), custom_call_target="tpu_custom_call" | custom-call | tf_op jit(solution)/shard_map/prep/pallas_call | solution.py:95
  5.8 0.0 copy-start
  5.8 109.2 %all_to_all.16.x_ref = bf16[128,32,1024]{2,1,0:T(8,128)(2,1)S(1)} all-to-all(bf16[128,32,1024]{2,1,0:T(8,128)(2,1)S(1)} %bitcast.7), channel_id=1, replica_groups=mesh['group'=64,'blk'=2] {'group','blk'}, dimensions={0} | all-to-all | bytes 16777216 | tf_op jit(solution)/shard_map/all_to_all | solution.py:224
  115.0 0.0 copy-done
  115.0 11.0 %near.1 = f32[16,8,32]{2,1,0:T(8,128)S(1)} custom-call(bf16[128,32,1024]{2,1,0:T(8,128)(2,1)S(1)} %all_to_all.16.x_ref), custom_call_target="tpu_custom_call" | custom-call | tf_op jit(solution)/shard_map/near/pallas_call | solution.py:168
  126.0 14.2 %all_to_all.17 = f32[128,1,32]{2,1,0:T(1,128)} all-to-all(f32[128,1,32]{2,1,0:T(1,128)S(1)} %bitcast.8), channel_id=1, replica_groups=mesh['group'=64,'blk'=2] {'group','blk'}, dimensions={0} | all-to-all | bytes 32768 | tf_op jit(solution)/shard_map/all_to_all | solution.py:226
  140.2 1.8 %pick.1 = f32[1,2048]{1,0:T(1,128)} custom-call(f32[128,32]{1,0:T(8,128)} %bitcast.9, s32[1,2048]{1,0:T(1,128)} %copy-done), custom_call_target="tpu_custom_call" | custom-call | tf_op jit(solution)/shard_map/pick/pallas_call | solution.py:208
Async XLA Ops:
  5.8 109.3 %copy-start = (s32[1,2048]{1,0:T(1,128)}, s32[1,2048]{1,0:T(1,128)S(1)}, u32[]{:S(2)}) copy-start(s32[1,2048]{1,0:T(1,128)S(1)} %get-tuple-element.8.target_ref) | copy-start | bytes 24580
